TPU v7x, 32 devices: a whole 2x2x4 slice. The times are simulated.
32 devices in a mesh: row: 4 (over y, x), col: 8 (over z, core).
Axes of the slice: x: 2, y: 2, z: 4, core: 2. Of those that a mesh axis runs over, the one named last changes fastest.
Arguments:
- factors: bfloat16 [16384, 2048], P(('row', 'col')), may hold values from -6 to 6
- dressed: bfloat16 [16384, 2048], P(('col', 'row')), may hold values from -0.125 to 0.125
- amplitudes: float32 [544, 512, 512], P(('row', 'col')), may hold values from -2.4 to 2.4
- fock_vv: float32 [512, 512], replicated, as said below
- occ_energy: float32 [32], replicated, may hold values from -2 to -0.3
- pair_list: int32 [528, 2], replicated, may hold values from 0 to 31, as said below
- owner_map: int32 [528], replicated, may hold values from 0 to 31, as said below
Outputs:
- updated: float32 [544, 512, 512], P(('row', 'col'))
- pair_energy: float32 [544], P(('row', 'col'))
Inputs may be any that keep to these rules, and one draw needn't show every extreme that they name: `pair_list`: every unordered pair of occupied orbitals appears exactly once, as i <= j. `owner_map`: each device owns 528 // 32 or 17 pairs, and some device owns exactly 17. `fock_vv`: Symmetric; its diagonal lies between 1 and 3.
All inputs are finite; a program needn't handle non-finite values.
Results may differ from a plain program's by a relative error of at most 0.0041.
Values may be sent and summed in bfloat16 or wider, within the bound.
A program may use at most 192 MiB of HBM per device.

v0:
```python
import jax
import jax.numpy as jnp
from jax import lax
from jax.sharding import PartitionSpec as P


def local(factors, dressed, amplitudes, fock_vv, occ_energy, pair_list, owner_map):
    highest = lax.Precision.HIGHEST
    row_count = lax.axis_size("row")
    col_count = lax.axis_size("col")
    device_count = row_count * col_count
    occ_total = occ_energy.shape[0]
    virtual = fock_vv.shape[0]
    occ_row = occ_total // row_count
    occ_col = occ_total // col_count
    capacity = amplitudes.shape[0]
    col_panel = lax.all_gather(dressed, "row", axis=0, tiled=True)
    tile_grid = lax.dot_general(
        lax.all_gather(factors, "col", axis=0, tiled=True),
        col_panel,
        (((1,), (1,)), ((), ())),
        preferred_element_type=jnp.float32,
    )
    tile_grid = tile_grid.reshape(occ_row, virtual, occ_col, virtual).transpose(0, 2, 1, 3)
    first_orbs = lax.axis_index("row") * occ_row + jnp.arange(occ_row, dtype=jnp.int32)
    second_orbs = lax.axis_index("col") * occ_col + jnp.arange(occ_col, dtype=jnp.int32)
    below = (first_orbs[:, None] > second_orbs[None, :])[:, :, None, None]
    on_diagonal = (first_orbs[:, None] == second_orbs[None, :])[:, :, None, None]
    flipped = jnp.swapaxes(tile_grid, 2, 3)
    oriented = jnp.where(
        on_diagonal, 0.5 * (tile_grid + flipped), jnp.where(below, flipped, tile_grid)
    )
    oriented = oriented.astype(jnp.bfloat16).reshape(occ_row * occ_col, virtual, virtual)
    first_pair = pair_list[:, 0]
    second_pair = pair_list[:, 1]
    received = lax.all_to_all(oriented, ("row", "col"), split_axis=1, concat_axis=0, tiled=True)
    forward = first_pair // occ_row * col_count + second_pair // occ_col
    backward = second_pair // occ_row * col_count + first_pair // occ_col
    forward = (forward * occ_row + first_pair % occ_row) * occ_col + second_pair % occ_col
    backward = (backward * occ_row + second_pair % occ_row) * occ_col + first_pair % occ_col
    symmetric = (
        received[forward].astype(jnp.float32) + received[backward].astype(jnp.float32)
    ).astype(jnp.bfloat16)
    positions = jnp.arange(pair_list.shape[0], dtype=jnp.int32)
    same_owner = owner_map[:, None] == owner_map[None, :]
    earlier = positions[:, None] > positions[None, :]
    slot_index = jnp.sum((same_owner & earlier).astype(jnp.int32), axis=1)
    target = owner_map * capacity + slot_index
    slots_all = jnp.arange(device_count * capacity, dtype=jnp.int32)
    filled = (target[None, :] == slots_all[:, None]).astype(jnp.int32)
    occupied_slot = jnp.sum(filled, axis=1) > 0
    pair_at = jnp.sum(filled * positions[None, :], axis=1)
    outgoing = jnp.where(
        occupied_slot[:, None, None], symmetric[pair_at], jnp.zeros((), jnp.bfloat16)
    )
    owned = lax.all_to_all(outgoing, ("row", "col"), split_axis=0, concat_axis=1, tiled=True)
    own_index = lax.axis_index("row") * col_count + lax.axis_index("col")
    base_slot = own_index * capacity
    mine_pair = lax.dynamic_slice_in_dim(pair_at, base_slot, capacity)
    mine_live = lax.dynamic_slice_in_dim(occupied_slot, base_slot, capacity)
    pair_orbs = pair_list[mine_pair]
    pair_shift = occ_energy[pair_orbs[:, 0]] + occ_energy[pair_orbs[:, 1]]
    source_part = owned.astype(jnp.float32)
    residual = source_part + jnp.einsum("ac,scb->sab", fock_vv, amplitudes, precision=highest)
    residual = residual + jnp.einsum("sac,cb->sab", amplitudes, fock_vv, precision=highest)
    residual = residual - pair_shift[:, None, None] * amplitudes
    orbital_level = jnp.diagonal(fock_vv)
    denominator = (
        orbital_level[None, :, None] + orbital_level[None, None, :] - pair_shift[:, None, None]
    )
    updated = jnp.where(mine_live[:, None, None], amplitudes - residual / denominator, 0.0)
    energy = jnp.where(mine_live, jnp.mean(source_part * updated, axis=(1, 2)), 0.0)
    return (updated, energy)


def solution(mesh):
    return jax.shard_map(
        local,
        mesh=mesh,
        in_specs=(
            P(("row", "col"), None),
            P(("col", "row"), None),
            P(("row", "col"), None, None),
            P(),
            P(),
            P(),
            P(),
        ),
        out_specs=(P(("row", "col"), None, None), P(("row", "col"))),
        check_vma=False,
    )
```

profile of v0, /device:TPU:0, one launch (start us, length us, event | category | flops | bytes accessed | tf_op | source)
XLA Modules:
  0.0 1254.6 jit_solution(17124063720525680397)
XLA Ops:
  7.2 0.0 copy-start
  7.2 0.0 all-gather.5.cloned.1.call-start
  7.2 0.7 all-gather.5.cloned.1.call-update
  7.9 0.0 all-gather.3.cloned.1.call-start
  8.0 0.7 all-gather.3.cloned.1.call-update
  8.7 0.1 broadcast_compare_fusion.1
  8.8 91.4 %all-gather.5.cloned.1.call-done = bf16[2048,2048]{1,0:T(8,128)(2,1)} async-done(((bf16[512,2048]{1,0:T(8,128)(2,1)}), bf16[2048,2048]{1,0:T(8,128)(2,1)}) %all-gather.5.cloned.1.call-update) | async-done | bytes 8388624 | tf_op jit(solution)/shard_map/all_gather | solution.py:17
  100.2 152.7 %all-gather.3.cloned.1.call-done = bf16[4096,2048]{1,0:T(8,128)(2,1)} async-done(((bf16[512,2048]{1,0:T(8,128)(2,1)}), bf16[4096,2048]{1,0:T(8,128)(2,1)}) %all-gather.3.cloned.1.call-update) | async-done | bytes 16777232 | tf_op jit(solution)/shard_map/all_gather | solution.py:19
  252.9 43.3 %fusion.21 = f32[4096,2048]{1,0:T(8,128)} fusion(bf16[4096,2048]{1,0:T(8,128)(2,1)} %all-gather.3.cloned.1.call-done, bf16[2048,2048]{1,0:T(8,128)(2,1)} %all-gather.5.cloned.1.call-done), kind=kOutput, calls=%fused_computation.79 | convolution fusion | flops 34359738368 | bytes 58720256 | tf_op jit(solution)/shard_map/dot_general | solution.py:18
  296.2 39.6 %reshape.133 = f32[8,512,4,512]{3,2,1,0:T(4,128)} reshape(f32[4096,2048]{1,0:T(8,128)} %fusion.21) | data formatting | bytes 67108864 | tf_op jit(solution)/shard_map/reshape | solution.py:24
  335.8 37.9 %copy.55 = f32[8,512,4,512]{1,3,2,0:T(8,128)} copy(f32[8,512,4,512]{3,2,1,0:T(4,128)} %reshape.133) | data formatting | bytes 67108864 | tf_op jit(solution)/shard_map/reshape | solution.py:24
  373.7 31.4 %fusion.2 = bf16[8,4,512,512]{3,2,1,0:T(8,128)(2,1)} fusion(f32[8,512,4,512]{1,3,2,0:T(8,128)} %copy.55, f32[8,512,4,512]{3,2,1,0:T(4,128)} %reshape.133, pred[8,4]{1,0:T(8,128)(4,1)S(1)} %get-tuple-element.19, pred[8,4]{1,0:T(8,128)(4,1)S(1)} %get-tuple-element.18), kind=kLoop, calls=%fused_computation.11 | loop fusion | flops 41943040 | bytes 83886144 | tf_op jit(solution)/shard_map/convert_element_type | solution.py:33
  405.1 18.7 %copy.56 = bf16[32,512,512]{2,0,1:T(8,128)(2,1)} copy(bf16[32,512,512]{2,1,0:T(8,128)(2,1)} %bitcast.50) | data formatting | bytes 33554432 | tf_op jit(solution)/shard_map/reshape | solution.py:33
  423.8 0.0 copy-start.2
  423.8 0.0 copy-start.3
  423.8 4.0 all-to-all-start
  427.8 0.0 copy-done.2
  427.9 0.3 convert_reduce_fusion.1
  428.1 0.3 convert_reduce_fusion
  428.5 0.0 copy-done.3
  428.5 0.1 fusion.18
  428.6 363.9 %all-to-all-done = bf16[32,512,512]{2,0,1:T(8,128)(2,1)} async-done(((bf16[32,512,512]{2,0,1:T(8,128)(2,1)}), bf16[32,512,512]{2,0,1:T(8,128)(2,1)}, u32[]{:S(2)}, u32[]{:S(2)}) %all-to-all-start) | async-done | bytes 16777248 | tf_op jit(solution)/shard_map/all_to_all | solution.py:36
  792.5 18.4 %copy.58 = bf16[32,32,16,512]{3,2,1,0:T(8,128)(2,1)} copy(bf16[32,32,16,512]{3,1,2,0:T(8,128)(2,1)} %bitcast.5) | data formatting | bytes 33554432 | tf_op jit(solution)/shard_map/all_to_all | solution.py:36
  810.9 25.4 %gather_fusion.1 = bf16[528,16,512]{2,1,0:T(8,128)(2,1)} fusion(bf16[1024,16,512]{2,1,0:T(8,128)(2,1)} %bitcast.48, s32[1024]{0:T(1024)S(1)} %get-tuple-element.22), kind=kCustom, calls=%fused_computation.1 | custom fusion | bytes 17303616 | tf_op jit(solution)/shard_map/gather | solution.py:42
  836.4 35.7 %gather_fusion = bf16[528,16,512]{2,1,0:T(8,128)(2,1)} fusion(bf16[1024,16,512]{2,1,0:T(8,128)(2,1)} %bitcast.49, s32[1024]{0:T(1024)S(1)} %get-tuple-element.23), kind=kCustom, calls=%fused_computation | custom fusion | bytes 17303616 | tf_op jit(solution)/shard_map/gather | solution.py:42
  872.1 10.8 add_convert_fusion
  882.9 23.1 %gather_fusion.2 = bf16[544,16,512]{2,1,0:T(8,128)(2,1)} fusion(bf16[528,16,512]{2,1,0:T(8,128)(2,1)} %add_convert_fusion, s32[1024]{0:T(1024)S(1)} %pad_clamp_fusion.3), kind=kCustom, calls=%fused_computation.2 | custom fusion | bytes 17827968 | tf_op jit(solution)/shard_map/gather | solution.py:54
  906.0 8.1 broadcast_select_fusion
  914.1 4.1 all-to-all-start.1
  918.2 0.1 copy.63
  918.3 0.0 copy-start.1
  918.4 18.2 %copy.65 = f32[17,512,512]{1,2,0:T(8,128)} copy(f32[17,512,512]{2,1,0:T(8,128)} %param.9) | data formatting | bytes 35651584 | tf_op args[2]
  936.6 0.1 dynamic_slice.6
  936.6 0.1 compare_select_fusion.5
  936.7 0.6 gather_fusion.3
  937.3 0.2 fusion.13
  937.5 0.0 copy-done.1
  937.5 0.7 gather_fusion.4
  938.2 0.7 gather_fusion.5
  938.9 0.0 copy-done
  938.9 4.5 gather_fusion.6
  943.5 0.1 broadcast_add_fusion
  943.6 38.3 %fusion.9 = f32[17,512,512]{1,2,0:T(8,128)} fusion(f32[17,512,512]{2,1,0:T(8,128)} %param.9, f32[512,512]{1,0:T(8,128)S(1)} %copy-done), kind=kOutput, calls=%fused_computation.28 | convolution fusion | flops 27380416512 | bytes 36700160 | tf_op jit(solution)/shard_map/sac,cb->sab/dot_general | solution.py:65
  981.9 132.4 %all-to-all-done.1 = bf16[544,16,512]{2,1,0:T(8,128)(2,1)} async-done(((bf16[544,16,512]{2,1,0:T(8,128)(2,1)}), bf16[544,16,512]{2,1,0:T(8,128)(2,1)}, u32[]{:S(2)}, u32[]{:S(2)}) %all-to-all-start.1) | async-done | bytes 8912928 | tf_op jit(solution)/shard_map/all_to_all | solution.py:56
  1114.3 12.5 convert_bitcast_fusion
  1126.9 12.8 %copy.59 = f32[17,32,16,512]{3,2,1,0:T(8,128)} copy(f32[17,32,16,512]{3,2,0,1:T(8,128)} %convert_bitcast_fusion) | data formatting | bytes 35651584 | tf_op jit(solution)/shard_map/convert_element_type | solution.py:63
  1139.7 18.2 %copy.61 = f32[17,512,512]{1,2,0:T(8,128)} copy(f32[17,512,512]{2,1,0:T(8,128)} %bitcast.47) | data formatting | bytes 35651584 | tf_op jit(solution)/shard_map/convert_element_type | solution.py:63
  1157.9 70.8 %multiply_reduce_fusion = (f32[17]{0:T(128)S(1)}, f32[17,512,512]{1,2,0:T(8,128)}) fusion(f32[17,512,512]{1,2,0:T(8,128)} %copy.61, f32[17,512,512]{1,2,0:T(8,128)} %copy.65, f32[512,512]{0,1:T(8,128)S(1)} %broadcast_add_fusion, f32[17]{0:T(128)S(1)} %add.185, f32[17,512,512]{1,2,0:T(8,128)} %fusion.9, f32[17,512,512]{2,1,0:T(8,128)} %param.9, ...), kind=kOutput, calls=%fused_computation.19 | convolution fusion | flops 27424980992 | bytes 91226264 | tf_op jit(solution)/shard_map/ac,scb->sab/dot_general | solution.py:64
  1228.8 18.2 %copy.67 = f32[17,512,512]{2,1,0:T(8,128)} copy(f32[17,512,512]{1,2,0:T(8,128)} %get-tuple-element.21) | data formatting | bytes 35651584
  1247.0 0.6 multiply_select_fusion
  (11 shorter events, 0.1 us)
Async XLA Ops:
  7.2 931.7 %copy-start = (f32[512,512]{1,0:T(8,128)S(1)}, f32[512,512]{1,0:T(8,128)}, u32[]{:S(2)}) copy-start(f32[512,512]{1,0:T(8,128)} %param.10) | copy-start | bytes 3145732
  7.2 93.0 %all-gather.5.cloned.1.call-start = ((), (), s32[]{:S(2)}) async-start(), calls=%async_computation.3 | async-start | bytes 10485760 | tf_op jit(solution)/shard_map/all_gather | solution.py:17
  7.9 245.0 %all-gather.3.cloned.1.call-start = ((), (), s32[]{:S(2)}) async-start(), calls=%async_computation.2 | async-start | bytes 18874368 | tf_op jit(solution)/shard_map/all_gather | solution.py:19
  423.8 4.0 copy-start.2
  423.8 4.7 copy-start.3
  423.8 368.7 %all-to-all-start = ((bf16[32,512,512]{2,0,1:T(8,128)(2,1)}), bf16[32,512,512]{2,0,1:T(8,128)(2,1)}, u32[]{:S(2)}, u32[]{:S(2)}) async-start(bf16[32,512,512]{2,0,1:T(8,128)(2,1)} %copy.56), calls=%async_computation | async-start | bytes 33554432 | tf_op jit(solution)/shard_map/all_to_all | solution.py:36
  914.1 200.2 %all-to-all-start.1 = ((bf16[544,16,512]{2,1,0:T(8,128)(2,1)}), bf16[544,16,512]{2,1,0:T(8,128)(2,1)}, u32[]{:S(2)}, u32[]{:S(2)}) async-start(bf16[544,16,512]{2,1,0:T(8,128)(2,1)} %broadcast_select_fusion), calls=%async_computation.1 | async-start | bytes 17825792 | tf_op jit(solution)/shard_map/all_to_all | solution.py:56
  918.3 19.1 %copy-start.1 = (f32[32]{0:T(128)S(1)}, f32[32]{0:T(128)}, u32[]{:S(2)}) copy-start(f32[32]{0:T(128)} %param.11) | copy-start | bytes 388
Sparse Core Ops, SparseCore 0:
  9.9 90.2 all-gather.4
  101.8 151.0 all-gather.2
where the time goes:
time: 1260 us; the launch traced here: 1250 us
  waiting for transfers between devices  742 us (59%)
  local copies, waits for them, and re-layouts  273 us (22%)
  matrix products  152 us (12%)
  other arithmetic  64.6 us (5%)
  between operations  14.4 us (1%)
    all_to_all x1, waiting for transfers between devices, local(): lax.all_to_all(oriented, ('row', 'col'), split_axis=1, concat_axis=0, til...  364 us
    all_gather x1, waiting for transfers between devices, local(): lax.all_gather(factors, 'col', axis=0, tiled=True)  153 us
    all_to_all x1, waiting for transfers between devices, local(): lax.all_to_all(outgoing, ('row', 'col'), split_axis=0, concat_axis=1, til...  132 us
    all_gather x1, waiting for transfers between devices, local(): col_panel = lax.all_gather(dressed, 'row', axis=0, tiled=True)  91.4 us
    reshape x2, local copies, waits for them, and re-layouts, local(): tile_grid.reshape(occ_row, virtual, occ_col, virtual).transpose(0, 2, 1, 3)  77.5 us
    dot_general x1, matrix products, local(): jnp.einsum('ac,scb->sab', fock_vv, amplitudes, precision=highest)  70.8 us
    dot_general x1, matrix products, local(): lax.dot_general(lax.all_gather(factors, 'col', axis=0, tiled=True), col_p...  43.3 us
    dot_general x1, matrix products, local(): jnp.einsum('sac,cb->sab', amplitudes, fock_vv, precision=highest)  38.3 us
  transfers between devices with their start and end apart: 4, of which 4 were waited for; matrix products, arithmetic and copies ran while one was open for 5% of the time, Pallas kernels for 0%

commit v1 on v0

v1 whole, which is shorter than its diff:
```python
import functools

import jax
import jax.numpy as jnp
from jax import lax
from jax.experimental import pallas as pl
from jax.experimental.pallas import tpu as pltpu
from jax.sharding import PartitionSpec as P

MESH = pl.DeviceIdType.MESH
MIB = 1024 * 1024


def split_axis(size):
    return (size // 2, 2) if size % 2 == 0 else (size, 1)


def when(conds, body):
    if not conds:
        body()
        return
    total = conds[0]
    for extra in conds[1:]:
        total = jnp.logical_and(total, extra)
    pl.when(total)(body)


def neighbours(position, size):
    if size == 1:
        return []
    if size == 2:
        return [(0, 1 - position, [])]
    return [
        (0, position + 1, [position + 1 < size]),
        (1, position - 1, [position >= 1]),
    ]


def arrivals(position, size, step):
    if size == 2:
        return [(1 - position, None, [])]
    return [
        (position - step, 0, [position - step >= 0]),
        (position + step, 1, [position + step < size]),
    ]


def gather_kernel(row_count, col_count, left_ref, right_ref, left_all, right_all, send_sem, recv_sem, own_sem):
    highs, lows = split_axis(row_count)
    lines, cores = split_axis(col_count)
    row, col = lax.axis_index("row"), lax.axis_index("col")
    high, low = row // lows, row % lows
    line, core = col // cores, col % cores
    place = {"line": line, "low": low, "high": high, "core": core}
    extent = {"line": lines, "low": lows, "high": highs, "core": cores}
    arrays = (
        (left_ref, left_all, ("line", "low", "high")),
        (right_ref, right_all, ("line", "high", "low")),
    )

    def device(at):
        return (at["high"] * lows + at["low"], at["line"] * cores + at["core"])

    def block_of(which, at):
        r, c = device(at)
        return r * col_count + c if which == 0 else c * row_count + r

    barrier = pltpu.get_barrier_semaphore()
    for axis in ("line", "low", "high", "core"):
        for _, other, conds in neighbours(place[axis], extent[axis]):
            when(conds, lambda axis=axis, other=other: pl.semaphore_signal(
                barrier, inc=1, device_id=device({**place, axis: other}), device_id_type=MESH))
    peers = 0
    for axis in ("line", "low", "high", "core"):
        for _, other, conds in neighbours(place[axis], extent[axis]):
            peers += conds[0].astype(jnp.int32) if conds else 1
    pl.semaphore_wait(barrier, peers)

    sent = []

    def plan(which, origin, stage, travel, guard, own=False):
        source, target, order = arrays[which]
        hops = []
        for later in range(stage, len(order)):
            axis = order[later]
            for way, other, conds in neighbours(place[axis], extent[axis]):
                if later == stage and not own and (extent[axis] == 2 or way != travel):
                    continue
                hops.append((axis, 2 * later + way, other, conds))
        for _, other, conds in neighbours(core, cores):
            hops.append(("core", 6, other, conds))
        copies = []
        for axis, lane, other, conds in hops:
            def make(axis=axis, lane=lane, other=other):
                blk = block_of(which, origin)
                return pltpu.make_async_remote_copy(
                    src_ref=source if own else target.at[blk],
                    dst_ref=target.at[blk],
                    send_sem=send_sem.at[which, blk, lane],
                    recv_sem=recv_sem.at[which, blk],
                    device_id=device({**place, axis: other}),
                    device_id_type=MESH,
                )

            copies.append((conds, make))
            sent.append((guard + conds, make))
        return copies

    def arrived(which, blk):
        target = arrays[which][1]
        pltpu.make_async_remote_copy(
            src_ref=target.at[blk], dst_ref=target.at[blk],
            send_sem=send_sem.at[which, blk, 0], recv_sem=recv_sem.at[which, blk],
            device_id=device(place), device_id_type=MESH,
        ).wait_recv()

    own_copies = []
    for which in range(2):
        for conds, make in plan(which, place, 0, None, [], own=True):
            when(conds, lambda: make().start())
        source, target, _ = arrays[which]
        copy = pltpu.make_async_copy(source, target.at[block_of(which, place)], own_sem.at[which])
        copy.start()
        own_copies.append(copy)

    def take(which, origin, stage, travel, guard):
        copies = plan(which, origin, stage, travel, guard)

        def body():
            arrived(which, block_of(which, origin))
            for conds, make in copies:
                when(conds, lambda: make().start())

        when(guard, body)

    def distance(step):
        if step == 0:
            return [(line, None, [])]
        return arrivals(line, lines, step)

    for turn in range(lines + 2):
        if 1 <= turn < lines:
            for origin, travel, guard in distance(turn):
                for which in range(2):
                    take(which, {**place, "line": origin}, 0, travel, guard)
        if 0 <= turn - 1 < lines:
            for from_line, _, guard in distance(turn - 1):
                for step in range(1, max(highs, lows)):
                    for which in range(2):
                        axis = arrays[which][2][1]
                        if step >= extent[axis]:
                            continue
                        for origin, travel, more in arrivals(place[axis], extent[axis], step):
                            take(which, {**place, "line": from_line, axis: origin}, 1, travel, guard + more)
        if 0 <= turn - 2 < lines:
            for from_line, _, guard in distance(turn - 2):
                for offset in range(max(highs, lows)):
                    for step in range(1, max(highs, lows)):
                        for which in range(2):
                            first, last = arrays[which][2][1:]
                            if offset >= extent[first] or step >= extent[last]:
                                continue
                            shifted = (place[first] + offset) % extent[first]
                            for origin, travel, more in arrivals(place[last], extent[last], step):
                                take(which, {**place, "line": from_line, first: shifted, last: origin}, 2, travel, guard + more)

    if cores > 1:
        def from_sibling(index, carry):
            at = {
                "high": index // (lows * lines),
                "low": index // lines % lows,
                "line": index % lines,
                "core": 1 - core,
            }
            for which in range(2):
                arrived(which, block_of(which, at))
            return carry

        lax.fori_loop(0, highs * lows * lines, from_sibling, 0)
    for conds, make in sent:
        when(conds, lambda: make().wait_send())
    for copy in own_copies:
        copy.wait()


def gather(factors, dressed):
    row_count, col_count = lax.axis_size("row"), lax.axis_size("col")
    devices = row_count * col_count
    rows, depth = factors.shape
    whole = jax.ShapeDtypeStruct((devices, rows, depth), factors.dtype)
    return pl.pallas_call(
        functools.partial(gather_kernel, row_count, col_count),
        out_shape=(whole, whole),
        in_specs=[pl.BlockSpec(memory_space=pl.ANY)] * 2,
        out_specs=(pl.BlockSpec(memory_space=pl.ANY), pl.BlockSpec(memory_space=pl.ANY)),
        scratch_shapes=[
            pltpu.SemaphoreType.DMA((2, devices, 7)),
            pltpu.SemaphoreType.DMA((2, devices)),
            pltpu.SemaphoreType.DMA((2,)),
        ],
        compiler_params=pltpu.CompilerParams(
            collective_id=0, has_side_effects=True, vmem_limit_bytes=4 * MIB
        ),
    )(factors, dressed)


def products(l_i, y_j, y_i, l_j):
    contract = (((1,), (1,)), ((), ()))
    forward = lax.dot_general(l_i[0], y_j[0], contract, preferred_element_type=jnp.float32)
    backward = lax.dot_general(y_i[0], l_j[0], contract, preferred_element_type=jnp.float32)
    return forward, backward


def partial_kernel(first, second, live, shift, l_i, y_j, y_i, l_j, sums):
    forward, backward = products(l_i, y_j, y_i, l_j)
    sums[0, 0] = forward
    sums[0, 1] = backward


def pair_kernel(earlier, first, second, live, shift, l_i, y_j, y_i, l_j, amp, coupling, level_col, level_row, *rest):
    out, energy = rest[earlier:]
    slot = pl.program_id(0)
    forward, backward = products(l_i, y_j, y_i, l_j)
    for sums in rest[:earlier]:
        forward = forward + sums[0, 0]
        backward = backward + sums[0, 1]
    apart = forward.astype(jnp.bfloat16).astype(jnp.float32) + backward.astype(jnp.bfloat16).astype(jnp.float32)
    same = first[slot] == second[slot]
    source = jnp.where(same, forward + backward, apart).astype(jnp.bfloat16).astype(jnp.float32)
    current = amp[0].astype(jnp.bfloat16)
    mixed = jnp.dot(coupling[...], current, preferred_element_type=jnp.float32)
    mixed = mixed + jnp.dot(current, coupling[...], preferred_element_type=jnp.float32)
    denominator = level_col[...] + level_row[...] - shift[slot]
    updated = jnp.where(live[slot] > 0, -(source + mixed) / denominator, 0.0)
    out[0] = updated
    total = jnp.sum(source * updated) / (updated.shape[0] * updated.shape[1])
    energy[...] = jnp.full(energy.shape, total, jnp.float32)


def local(factors, dressed, amplitudes, fock_vv, occ_energy, pair_list, owner_map):
    col_count = lax.axis_size("col")
    capacity = amplitudes.shape[0]
    virtual = fock_vv.shape[0]
    occupied = occ_energy.shape[0]
    depth = factors.shape[1]
    passes = 1 if lax.axis_size("row") * col_count <= 32 else 2
    depth = depth // passes

    own_index = lax.axis_index("row") * col_count + lax.axis_index("col")
    positions = jnp.arange(pair_list.shape[0], dtype=jnp.int32)
    mine = owner_map == own_index
    rank = jnp.sum((mine[None, :] & (positions[:, None] > positions[None, :])).astype(jnp.int32), axis=1)
    hit = mine[None, :] & (rank[None, :] == jnp.arange(capacity, dtype=jnp.int32)[:, None])
    live = jnp.sum(hit.astype(jnp.int32), axis=1)
    pair_orbs = jnp.sum(jnp.where(hit[:, :, None], pair_list[None, :, :], 0), axis=1)
    first, second = pair_orbs[:, 0], pair_orbs[:, 1]
    shift = occ_energy[first] + occ_energy[second]

    level = jnp.diagonal(fock_vv)
    off = jnp.where(jnp.eye(virtual, dtype=jnp.bool_), 0.0, fock_vv).astype(jnp.bfloat16)

    def panel(pick):
        return pl.BlockSpec((1, virtual, depth), lambda s, f, g, *_: ((f, g)[pick][s], 0, 0))

    def fixed(*shape):
        return pl.BlockSpec(shape, lambda s, *_: (0,) * len(shape))

    def per_slot(*shape):
        return pl.BlockSpec((1,) + shape, lambda s, *_: (s,) + (0,) * len(shape))

    def run(kernel, panels, others, other_specs, out_shape, out_specs):
        return pl.pallas_call(
            kernel,
            out_shape=out_shape,
            grid_spec=pltpu.PrefetchScalarGridSpec(
                num_scalar_prefetch=4,
                grid=(capacity,),
                in_specs=[panel(0), panel(1), panel(0), panel(1), *other_specs],
                out_specs=out_specs,
            ),
            compiler_params=pltpu.CompilerParams(vmem_limit_bytes=48 * MIB),
            cost_estimate=pl.CostEstimate(
                flops=4 * capacity * virtual * virtual * (depth + virtual),
                bytes_accessed=8 * capacity * virtual * (depth + virtual),
                transcendentals=0,
            ),
        )(first, second, live, shift, *panels, *others)

    partial = []
    for part in range(passes):
        at = slice(part * depth, (part + 1) * depth)
        pieces = (factors, dressed) if passes == 1 else (factors[:, at], dressed[:, at])
        if partial:
            pieces = lax.optimization_barrier((*pieces, partial[-1]))
            partial[-1] = pieces[2]
        left_all, right_all = (whole.reshape(occupied, virtual, depth) for whole in gather(*pieces[:2]))
        panels = (left_all, right_all, right_all, left_all)
        if part < passes - 1:
            shape = (2, virtual, virtual)
            partial.append(run(
                partial_kernel, panels, (), (),
                jax.ShapeDtypeStruct((capacity,) + shape, jnp.float32), per_slot(*shape)))
    updated, energy = run(
        functools.partial(pair_kernel, len(partial)),
        panels,
        (amplitudes, off, level[:, None], level[None, :], *partial),
        [
            per_slot(virtual, virtual), fixed(virtual, virtual), fixed(virtual, 1), fixed(1, virtual),
            *[per_slot(2, virtual, virtual)] * len(partial),
        ],
        (
            jax.ShapeDtypeStruct(amplitudes.shape, jnp.float32),
            jax.ShapeDtypeStruct((capacity, 8, 128), jnp.float32),
        ),
        (per_slot(virtual, virtual), per_slot(8, 128)),
    )
    return updated, energy[:, 0, 0]


def solution(mesh):
    return jax.shard_map(
        local,
        mesh=mesh,
        in_specs=(
            P(("row", "col"), None),
            P(("col", "row"), None),
            P(("row", "col"), None, None),
            P(),
            P(),
            P(),
            P(),
        ),
        out_specs=(P(("row", "col"), None, None), P(("row", "col"))),
        check_vma=False,
    )
```

time: 1260 us -> 639 us (0.51)
  waiting for transfers between devices: 742 us -> 0 us
  Pallas kernels: 0 us -> 622 us
  local copies, waits for them, and re-layouts: 273 us -> 12.8 us
  matrix products: 152 us -> 0 us
  other arithmetic: 64.6 us -> 1.8 us
  between operations: 14.4 us -> 0.76 us
    pallas_call x0 -> x2, Pallas kernels: none -> 622 us  [the longest x1 556 us: gather(): pl.pallas_call(functools.partial(gather_kernel, row_count, col_count), ou...]
    all_to_all x2 -> x0, waiting for transfers between devices: 496 us -> none  [the longest x1 364 us: local(): lax.all_to_all(oriented, ('row', 'col'), split_axis=1, concat_axis=0, til...]
    all_gather x2 -> x0, waiting for transfers between devices: 244 us -> none  [the longest x1 153 us: local(): lax.all_gather(factors, 'col', axis=0, tiled=True)]
    dot_general x3 -> x0, matrix products: 152 us -> none  [the longest x1 70.8 us: local(): jnp.einsum('ac,scb->sab', fock_vv, amplitudes, precision=highest)]
    reshape x3 -> x0, local copies, waits for them, and re-layouts: 96.2 us -> none  [the longest x2 77.5 us: local(): tile_grid.reshape(occ_row, virtual, occ_col, virtual).transpose(0, 2, 1, 3)]
    gather x7 -> x3, local copies, waits for them, and re-layouts: 90.7 us -> 10.3 us  [the longest x1 8.91 us: local(): level = jnp.diagonal(fock_vv)]
    convert_element_type x3 -> x1, other arithmetic: 54.8 us -> 0.08 us  [local(): jnp.where(jnp.eye(virtual, dtype=jnp.bool_), 0.0, fock_vv)]
    unnamed x11 -> x10, local copies, waits for them, and re-layouts: 36.6 us -> 1.61 us
  transfers between devices with their start and end apart: 4 -> 0, of which waited for: 4 -> 0; matrix products, arithmetic and copies ran while one was open for 5% -> 0% of each run, Pallas kernels for 0% -> 0%
where the time goes in v1:
time: 639 us; the launch traced here: 637 us
  Pallas kernels  622 us (97%)
  local copies, waits for them, and re-layouts  12.8 us (2%)
    pallas_call x1, Pallas kernels, gather(): pl.pallas_call(functools.partial(gather_kernel, row_count, col_count), ou...  556 us
    pallas_call x1, Pallas kernels, run(): pl.pallas_call(kernel, out_shape=out_shape, grid_spec=pltpu.PrefetchScala...  65.8 us

profile of v1, /device:TPU:0, one launch (start us, length us, event | category | flops | bytes accessed | tf_op | source)
XLA Modules:
  0.0 637.2 jit_solution(12043649316993506488)
XLA Ops:
  0.6 0.0 copy-start
  0.6 0.0 copy-start.3
  0.7 0.0 copy-start.4
  0.7 0.8 broadcast_compare_fusion
  1.5 0.0 copy-start.1
  1.5 8.9 %gather_fusion.2 = f32[512]{0:T(512)S(1)} fusion(f32[512,512]{1,0:T(8,128)} %param.10, s32[512]{0:T(512)S(1)} %bitcast.5), kind=kCustom, calls=%fused_computation.2 | custom fusion | bytes 8192 | tf_op jit(solution)/shard_map/jit(diagonal)/cond/branch_0_fun/gather | solution.py:259
  10.4 0.2 convert_reduce_fusion
  10.6 0.1 convert_reduce_fusion.1.live
  10.7 0.0 copy-done.4
  10.7 0.4 select_reduce_fusion
  11.1 0.2 fusion.3
  11.3 0.0 copy-done
  11.4 0.7 gather_fusion.1
  12.1 0.7 gather_fusion
  12.8 0.2 copy.13.level_col
  12.9 0.0 copy-done.3
  12.9 0.1 select_convert_fusion.coupling
  13.0 0.0 copy-done.1
  13.0 0.0 copy-start.2
  13.0 1.6 copy-done.2
  14.6 556.1 %shard_map.86 = (bf16[32,512,2048]{2,1,0:T(8,128)(2,1)}, bf16[32,512,2048]{2,1,0:T(8,128)(2,1)}) custom-call(bf16[512,2048]{1,0:T(8,128)(2,1)S(1)} %copy-done.1, bf16[512,2048]{1,0:T(8,128)(2,1)S(1)} %copy-done.2), custom_call_target="tpu_custom_call" | custom-call | tf_op jit(solution)/shard_map/pallas_call | solution.py:191
  570.7 65.8 %shard_map.87 = (f32[17,512,512]{2,1,0:T(8,128)}, f32[17,8,128]{2,1,0:T(8,128)S(1)}) custom-call(s32[17]{0:T(128)S(1)} %get-tuple-element.13.first, s32[17]{0:T(128)S(1)} %get-tuple-element.12.second, s32[17]{0:T(128)S(1)} %convert_reduce_fusion.1.live, f32[17]{0:T(128)S(1)} %add.21.shift, bf16[32,512,2048]{2,1,0:T(8,128)(2,1)} %get-tuple-element.6.l_i.l_j, ...), custom_call_target="tpu_custom_call" | custom-call | flops 45634027520 | bytes 178257920 | tf_op jit(solution)/shard_map/pallas_call | solution.py:272
  636.5 0.7 slice_reduce_fusion.2
  (4 shorter events, 0.0 us)
Async XLA Ops:
  0.6 10.7 %copy-start = (f32[32]{0:T(128)S(1)}, f32[32]{0:T(128)}, u32[]{:S(2)}) copy-start(f32[32]{0:T(128)} %param.11) | copy-start | bytes 388
  0.6 12.3 %copy-start.3 = (f32[512,512]{1,0:T(8,128)S(1)}, f32[512,512]{1,0:T(8,128)}, u32[]{:S(2)}) copy-start(f32[512,512]{1,0:T(8,128)} %param.10) | copy-start | bytes 3145732
  0.7 10.1 %copy-start.4 = (s32[528,2]{0,1:T(2,128)S(1)}, s32[528,2]{0,1:T(2,128)}, u32[]{:S(2)}) copy-start(s32[528,2]{0,1:T(2,128)} %param.12) | copy-start | bytes 12676
  1.5 11.6 %copy-start.1 = (bf16[512,2048]{1,0:T(8,128)(2,1)S(1)}, bf16[512,2048]{1,0:T(8,128)(2,1)}, u32[]{:S(2)}) copy-start(bf16[512,2048]{1,0:T(8,128)(2,1)} %left_ref.1) | copy-start | bytes 6291460
  13.0 1.6 copy-start.2

commit v2 on v1

--- a/solution.py
+++ b/solution.py
@@ -1,4 +1,5 @@
 import functools
+import itertools
 
 import jax
 import jax.numpy as jnp
@@ -45,7 +46,7 @@
     ]
 
 
-def gather_kernel(row_count, col_count, left_ref, right_ref, left_all, right_all, send_sem, recv_sem, own_sem):
+def gather_kernel(row_count, col_count, routes, left_ref, right_ref, left_all, right_all, send_sem, recv_sem, own_sem):
     highs, lows = split_axis(row_count)
     lines, cores = split_axis(col_count)
     row, col = lax.axis_index("row"), lax.axis_index("col")
@@ -53,17 +54,23 @@
     line, core = col // cores, col % cores
     place = {"line": line, "low": low, "high": high, "core": core}
     extent = {"line": lines, "low": lows, "high": highs, "core": cores}
-    arrays = (
-        (left_ref, left_all, ("line", "low", "high")),
-        (right_ref, right_all, ("line", "high", "low")),
-    )
+    rows = left_ref.shape[0]
+    share = rows * 2 // len(routes)
+    arrays = [
+        ((left_ref, right_ref)[side], (left_all, right_all)[side], side, part * share, order)
+        for side, part, order in routes
+    ]
 
     def device(at):
         return (at["high"] * lows + at["low"], at["line"] * cores + at["core"])
 
     def block_of(which, at):
         r, c = device(at)
-        return r * col_count + c if which == 0 else c * row_count + r
+        return r * col_count + c if arrays[which][2] == 0 else c * row_count + r
+
+    def piece(which, blk):
+        _, target, _, start, _ = arrays[which]
+        return target.at[blk, pl.ds(start, share)]
 
     barrier = pltpu.get_barrier_semaphore()
     for axis in ("line", "low", "high", "core"):
@@ -79,7 +86,7 @@
     sent = []
 
     def plan(which, origin, stage, travel, guard, own=False):
-        source, target, order = arrays[which]
+        source, _, _, start, order = arrays[which]
         hops = []
         for later in range(stage, len(order)):
             axis = order[later]
@@ -94,8 +101,8 @@
             def make(axis=axis, lane=lane, other=other):
                 blk = block_of(which, origin)
                 return pltpu.make_async_remote_copy(
-                    src_ref=source if own else target.at[blk],
-                    dst_ref=target.at[blk],
+                    src_ref=source.at[pl.ds(start, share)] if own else piece(which, blk),
+                    dst_ref=piece(which, blk),
                     send_sem=send_sem.at[which, blk, lane],
                     recv_sem=recv_sem.at[which, blk],
                     device_id=device({**place, axis: other}),
@@ -107,19 +114,19 @@
         return copies
 
     def arrived(which, blk):
-        target = arrays[which][1]
         pltpu.make_async_remote_copy(
-            src_ref=target.at[blk], dst_ref=target.at[blk],
+            src_ref=piece(which, blk), dst_ref=piece(which, blk),
             send_sem=send_sem.at[which, blk, 0], recv_sem=recv_sem.at[which, blk],
             device_id=device(place), device_id_type=MESH,
         ).wait_recv()
 
     own_copies = []
-    for which in range(2):
+    for which in range(len(arrays)):
         for conds, make in plan(which, place, 0, None, [], own=True):
             when(conds, lambda: make().start())
-        source, target, _ = arrays[which]
-        copy = pltpu.make_async_copy(source, target.at[block_of(which, place)], own_sem.at[which])
+        source, _, _, start, _ = arrays[which]
+        copy = pltpu.make_async_copy(
+            source.at[pl.ds(start, share)], piece(which, block_of(which, place)), own_sem.at[which])
         copy.start()
         own_copies.append(copy)
 
@@ -133,36 +140,25 @@
 
         when(guard, body)
 
-    def distance(step):
-        if step == 0:
-            return [(line, None, [])]
-        return arrivals(line, lines, step)
-
-    for turn in range(lines + 2):
-        if 1 <= turn < lines:
-            for origin, travel, guard in distance(turn):
-                for which in range(2):
-                    take(which, {**place, "line": origin}, 0, travel, guard)
-        if 0 <= turn - 1 < lines:
-            for from_line, _, guard in distance(turn - 1):
-                for step in range(1, max(highs, lows)):
-                    for which in range(2):
-                        axis = arrays[which][2][1]
-                        if step >= extent[axis]:
-                            continue
-                        for origin, travel, more in arrivals(place[axis], extent[axis], step):
-                            take(which, {**place, "line": from_line, axis: origin}, 1, travel, guard + more)
-        if 0 <= turn - 2 < lines:
-            for from_line, _, guard in distance(turn - 2):
-                for offset in range(max(highs, lows)):
-                    for step in range(1, max(highs, lows)):
-                        for which in range(2):
-                            first, last = arrays[which][2][1:]
-                            if offset >= extent[first] or step >= extent[last]:
-                                continue
-                            shifted = (place[first] + offset) % extent[first]
-                            for origin, travel, more in arrivals(place[last], extent[last], step):
-                                take(which, {**place, "line": from_line, first: shifted, last: origin}, 2, travel, guard + more)
+    def reach(axis):
+        near = [(0, place[axis], None, [])]
+        for step in range(1, extent[axis]):
+            near += [(step, *arrival) for arrival in arrivals(place[axis], extent[axis], step)]
+        return near
+
+    takes = []
+    for which in range(len(arrays)):
+        order = arrays[which][4]
+        for ways in itertools.product(*(reach(axis) for axis in order)):
+            hops = sum(way[0] for way in ways)
+            if hops == 0:
+                continue
+            stage = max(k for k in range(len(order)) if ways[k][0] > 0)
+            origin = {**place, **{axis: way[1] for axis, way in zip(order, ways)}}
+            guard = [cond for way in ways for cond in way[3]]
+            takes.append((hops, stage, len(takes), which, origin, ways[stage][2], guard))
+    for _, stage, _, which, origin, travel, guard in sorted(takes, key=lambda entry: entry[:3]):
+        take(which, origin, stage, travel, guard)
 
     if cores > 1:
         def from_sibling(index, carry):
@@ -172,7 +168,7 @@
                 "line": index % lines,
                 "core": 1 - core,
             }
-            for which in range(2):
+            for which in range(len(arrays)):
                 arrived(which, block_of(which, at))
             return carry
 
@@ -188,15 +184,18 @@
     devices = row_count * col_count
     rows, depth = factors.shape
     whole = jax.ShapeDtypeStruct((devices, rows, depth), factors.dtype)
+    routes = [(0, 0, ("line", "low", "high")), (1, 0, ("line", "high", "low"))]
+    if rows % 32 == 0 and devices <= 32:
+        routes += [(0, 1, ("low", "line", "high")), (1, 1, ("high", "line", "low"))]
     return pl.pallas_call(
-        functools.partial(gather_kernel, row_count, col_count),
+        functools.partial(gather_kernel, row_count, col_count, tuple(routes)),
         out_shape=(whole, whole),
         in_specs=[pl.BlockSpec(memory_space=pl.ANY)] * 2,
         out_specs=(pl.BlockSpec(memory_space=pl.ANY), pl.BlockSpec(memory_space=pl.ANY)),
         scratch_shapes=[
-            pltpu.SemaphoreType.DMA((2, devices, 7)),
-            pltpu.SemaphoreType.DMA((2, devices)),
-            pltpu.SemaphoreType.DMA((2,)),
+            pltpu.SemaphoreType.DMA((len(routes), devices, 7)),
+            pltpu.SemaphoreType.DMA((len(routes), devices)),
+            pltpu.SemaphoreType.DMA((len(routes),)),
         ],
         compiler_params=pltpu.CompilerParams(
             collective_id=0, has_side_effects=True, vmem_limit_bytes=4 * MIB
@@ -256,8 +255,9 @@
     first, second = pair_orbs[:, 0], pair_orbs[:, 1]
     shift = occ_energy[first] + occ_energy[second]
 
-    level = jnp.diagonal(fock_vv)
-    off = jnp.where(jnp.eye(virtual, dtype=jnp.bool_), 0.0, fock_vv).astype(jnp.bfloat16)
+    on_diagonal = jnp.eye(virtual, dtype=jnp.bool_)
+    level = jnp.sum(jnp.where(on_diagonal, fock_vv, 0.0), axis=0)
+    off = jnp.where(on_diagonal, 0.0, fock_vv).astype(jnp.bfloat16)
 
     def panel(pick):
         return pl.BlockSpec((1, virtual, depth), lambda s, f, g, *_: ((f, g)[pick][s], 0, 0))

time: 639 us -> 567 us (0.89)
  Pallas kernels: 622 us -> 558 us
  local copies, waits for them, and re-layouts: 12.8 us -> 3.88 us
    pallas_call x1, Pallas kernels: 556 us -> 490 us  [gather(): pl.pallas_call(functools.partial(gather_kernel, row_count, col_count, tup...]
    gather x1 -> x0, local copies, waits for them, and re-layouts: 8.91 us -> none  [local(): level = jnp.diagonal(fock_vv)]
where the time goes in v2:
time: 567 us; the launch traced here: 566 us
  Pallas kernels  558 us (98%)
    pallas_call x1, Pallas kernels, gather(): pl.pallas_call(functools.partial(gather_kernel, row_count, col_count, tup...  490 us
    pallas_call x1, Pallas kernels, run(): pl.pallas_call(kernel, out_shape=out_shape, grid_spec=pltpu.PrefetchScala...  67.5 us

profile of v2, /device:TPU:0, one launch (start us, length us, event | category | flops | bytes accessed | tf_op | source)
XLA Modules:
  0.0 566.3 jit_solution(1262702438390844444)
XLA Ops:
  0.6 0.0 copy-start
  0.6 0.0 copy-start.3
  0.7 0.0 copy-start.1
  0.7 0.8 broadcast_compare_fusion
  1.5 1.4 select_reduce_fusion
  2.9 0.2 convert_reduce_fusion
  3.1 0.1 convert_reduce_fusion.1.live
  3.2 1.1 select_reduce_fusion.1
  4.3 0.2 fusion.3
  4.5 0.0 copy-done
  4.5 0.7 gather_fusion.1
  5.2 0.7 gather_fusion
  5.9 0.2 copy.13.level_col
  6.1 0.0 copy-done.3
  6.1 0.1 select_convert_fusion.coupling
  6.2 0.0 copy-done.1
  6.2 0.0 copy-start.2
  6.2 1.6 copy-done.2
  7.8 490.3 %shard_map.86 = (bf16[32,512,2048]{2,1,0:T(8,128)(2,1)}, bf16[32,512,2048]{2,1,0:T(8,128)(2,1)}) custom-call(bf16[512,2048]{1,0:T(8,128)(2,1)S(1)} %copy-done.1, bf16[512,2048]{1,0:T(8,128)(2,1)S(1)} %copy-done.2), custom_call_target="tpu_custom_call" | custom-call | tf_op jit(solution)/shard_map/pallas_call | solution.py:190
  498.1 67.5 %shard_map.87 = (f32[17,512,512]{2,1,0:T(8,128)}, f32[17,8,128]{2,1,0:T(8,128)S(1)}) custom-call(s32[17]{0:T(128)S(1)} %get-tuple-element.13.first, s32[17]{0:T(128)S(1)} %get-tuple-element.12.second, s32[17]{0:T(128)S(1)} %convert_reduce_fusion.1.live, f32[17]{0:T(128)S(1)} %add.17.shift, bf16[32,512,2048]{2,1,0:T(8,128)(2,1)} %get-tuple-element.6.l_i.l_j, ...), custom_call_target="tpu_custom_call" | custom-call | flops 45634027520 | bytes 178257920 | tf_op jit(solution)/shard_map/pallas_call | solution.py:272
  565.5 0.7 slice_reduce_fusion.2
  (3 shorter events, 0.0 us)
Async XLA Ops:
  0.6 3.9 copy-start
  0.6 5.5 copy-start.3
  0.7 5.5 copy-start.1
  6.2 1.6 copy-start.2
